TPU v7x, 128 devices: a whole 4x4x4 slice. The times are simulated.
128 devices in a mesh: pool: 8 (over y, core), tp: 16 (over z, x).
Axes of the slice: x: 4, y: 4, z: 4, core: 2. Of those that a mesh axis runs over, the one named last changes fastest.
Arguments:
- queries: bfloat16 [64, 4, 24576], P('pool', None, 'tp'), may hold values from -18 to 18
- new_rows: bfloat16 [64, 4, 576], P('pool'), may hold values from -4 to 4
- prefill_latent: bfloat16 [8, 16, 44, 128, 512], P('pool', 'tp'), may hold values from -6 to 6
- prefill_rope: bfloat16 [8, 16, 44, 64, 128], P('pool', 'tp'), may hold values from -6 to 6
- lengths: int32 [8, 8], replicated, may hold values from 1 to 16384, 73728 in all within a row
- owner: int32 [8, 8], replicated, may hold values from 0 to 7, as said below
- pack_order: int32 [8, 16, 8], P('pool', 'tp'), may hold values from 0 to 7, each once within a row
- uk_weight: bfloat16 [128, 128, 512], P('tp'), may hold values from -0.5 to 0.5
- uv_weight: bfloat16 [128, 512, 128], P('tp'), may hold values from -1 to 1
- out_weight: bfloat16 [16384, 7168], P('tp'), may hold values from -0.1875 to 0.1875
Outputs:
- attended: bfloat16 [64, 4, 7168], P('pool')
Inputs may be any that keep to these rules, and one draw needn't show every extreme that they name: For every k, owner[:, k] names each decode group once, and the 8 entries of each row of owner differ. Each pack_order[p, t] is a permutation of the 8 sequences of group p. Every row of lengths sums to 73728 and its largest entry is exactly 16384.
All inputs are finite; a program needn't handle non-finite values.
Results may differ from a plain program's by a relative error of at most 0.02.
Values may be sent and summed in bfloat16 or wider, within the bound.
A program may use at most 128 MiB of HBM per device.

v0:
```python
import jax
import jax.numpy as jnp
from jax import lax
from jax.sharding import PartitionSpec as P

MAXLEN = 16384


MASKED = -1e30


def causal_mask(step_count):
    step_numbers = jnp.arange(step_count, dtype=jnp.int32)
    return step_numbers[None, :] <= step_numbers[:, None]


def new_row_scores(query_latent, query_rope, fresh_rows, score_scale):
    latent_width = query_latent.shape[-1]
    return (
        jnp.einsum(
            "gihd,gjd->gihj",
            query_latent,
            fresh_rows[..., :latent_width],
            preferred_element_type=jnp.float32,
        )
        + jnp.einsum(
            "gihe,gje->gihj",
            query_rope,
            fresh_rows[..., latent_width:],
            preferred_element_type=jnp.float32,
        )
    ) * score_scale


def attend(latents, rope_rows, query_latent, query_rope, row_lengths, fresh_rows, score_scale):
    tensor_count = lax.axis_size("tp")
    tensor_index = lax.axis_index("tp")
    source_count, block_slots, block_rows, latent_width = latents.shape
    step_count, head_count = (query_latent.shape[1], query_latent.shape[2])
    local_heads = head_count // tensor_count
    fresh_scores = new_row_scores(query_latent, query_rope, fresh_rows, score_scale)
    causal = causal_mask(step_count)[None, :, None, :]
    fresh_peak = jnp.max(jnp.where(causal, fresh_scores, MASKED), axis=3)
    flat_latent = query_latent.reshape(source_count, step_count * head_count, latent_width)
    flat_rope = query_rope.reshape(source_count, step_count * head_count, query_rope.shape[3])
    scores = (
        jnp.einsum("sqd,scnd->sqcn", flat_latent, latents, preferred_element_type=jnp.float32)
        + jnp.einsum("sqe,scen->sqcn", flat_rope, rope_rows, preferred_element_type=jnp.float32)
    ) * score_scale
    positions = (
        block_rows
        * (tensor_index + tensor_count * jnp.arange(block_slots, dtype=jnp.int32))[:, None]
        + jnp.arange(block_rows, dtype=jnp.int32)[None, :]
    )
    usable = (positions[None] < row_lengths[:, None, None])[:, None]
    cache_max = jnp.max(jnp.where(usable, scores, MASKED), axis=(2, 3)).reshape(
        source_count, step_count, head_count
    )
    maxima = jnp.maximum(lax.pmax(cache_max, "tp"), fresh_peak)
    weights = jnp.where(
        usable,
        jnp.exp(scores - maxima.reshape(source_count, step_count * head_count)[..., None, None]),
        0.0,
    )
    latent = jnp.einsum(
        "sqcn,scnd->sqd", weights.astype(jnp.bfloat16), latents, preferred_element_type=jnp.float32
    )
    latent = latent.reshape(source_count, step_count, head_count, latent_width)
    totals = jnp.sum(weights, axis=(2, 3)).reshape(source_count, step_count, head_count)
    latent, totals = lax.psum((latent, totals), "tp")
    latent = lax.dynamic_slice_in_dim(latent, tensor_index * local_heads, local_heads, 2)
    totals = lax.dynamic_slice_in_dim(totals, tensor_index * local_heads, local_heads, 2)
    maxima = lax.dynamic_slice_in_dim(maxima, tensor_index * local_heads, local_heads, 2)
    return (latent, totals, maxima)


def on_device(
    queries,
    new_rows,
    prefill_latent,
    prefill_rope,
    lengths,
    owner,
    pack_order,
    uk_weight,
    uv_weight,
    out_weight,
):
    tensor_count = lax.axis_size("tp")
    pool_count = lax.axis_size("pool")
    tensor_index = lax.axis_index("tp")
    pool_index = lax.axis_index("pool")
    local_heads, nope_width, latent_width = uk_weight.shape
    group_count, step_count = (queries.shape[0], queries.shape[1])
    rope_width = prefill_rope.shape[3]
    block_rows = prefill_latent.shape[3]
    stored_blocks = prefill_latent.shape[2]
    block_slots = MAXLEN // (block_rows * tensor_count)
    score_scale = (nope_width + rope_width) ** (-0.5)
    split_queries = queries.reshape(group_count, step_count, local_heads, nope_width + rope_width)
    local_latent = jnp.einsum(
        "gihn,hnd->gihd",
        split_queries[..., :nope_width],
        uk_weight,
        preferred_element_type=jnp.float32,
    ).astype(jnp.bfloat16)
    local_rope = split_queries[..., nope_width:]
    pool_numbers = jnp.arange(pool_count, dtype=jnp.int32)
    slot_numbers = jnp.arange(group_count, dtype=jnp.int32)
    arrives = (owner == pool_index).astype(jnp.int32)
    slot_of_source = jnp.sum(arrives * slot_numbers[None, :], axis=1)
    source_of_slot = jnp.sum(arrives * pool_numbers[:, None], axis=0)
    source_lengths = jnp.sum(arrives * lengths, axis=1)
    mine_latent = jnp.take(local_latent, slot_of_source, axis=0)
    mine_rope = jnp.take(local_rope, slot_of_source, axis=0)
    source_fresh = jnp.take(new_rows, slot_of_source, axis=0)
    prefill_lengths = lax.dynamic_index_in_dim(lengths, pool_index, 0, keepdims=False)
    counts = (
        jnp.maximum(
            (prefill_lengths + block_rows - 1) // block_rows - tensor_index + tensor_count - 1, 0
        )
        // tensor_count
    )
    packing = pack_order[0, 0]
    ordered = jnp.take(counts, packing)
    before = jnp.cumsum(ordered) - ordered
    starts = jnp.sum(
        (packing[:, None] == slot_numbers[None, :]).astype(jnp.int32) * before[:, None], axis=0
    )
    targets = lax.dynamic_index_in_dim(owner, pool_index, 0, keepdims=False)
    sends_to = (targets[None, :] == pool_numbers[:, None]).astype(jnp.int32)
    first_block = jnp.sum(sends_to * starts[None, :], axis=1)
    block_index = jnp.minimum(
        first_block[:, None] + jnp.arange(block_slots, dtype=jnp.int32)[None, :], stored_blocks - 1
    )
    latent_out = jnp.take(prefill_latent[0, 0], block_index, axis=0)
    rope_out = jnp.take(prefill_rope[0, 0], block_index, axis=0)
    source_latent, source_rope = (
        lax.all_gather(mine_latent, "tp", axis=2, tiled=True),
        lax.all_gather(mine_rope, "tp", axis=2, tiled=True),
    )
    latent_in, rope_in = (
        lax.all_to_all(latent_out, "pool", split_axis=0, concat_axis=0, tiled=True),
        lax.all_to_all(rope_out, "pool", split_axis=0, concat_axis=0, tiled=True),
    )
    latent, totals, maxima = attend(
        latent_in, rope_in, source_latent, source_rope, source_lengths, source_fresh, score_scale
    )
    latent = jnp.take(latent, source_of_slot, axis=0)
    totals = jnp.take(totals, source_of_slot, axis=0)
    maxima = jnp.take(maxima, source_of_slot, axis=0)
    fresh_scores = new_row_scores(local_latent, local_rope, new_rows, score_scale)
    causal = causal_mask(step_count)[None, :, None, :]
    fresh_weights = jnp.where(causal, jnp.exp(fresh_scores - maxima[..., None]), 0.0)
    latent = latent + jnp.einsum(
        "gihj,gjd->gihd", fresh_weights, new_rows[..., :latent_width].astype(jnp.float32)
    )
    totals = totals + jnp.sum(fresh_weights, axis=3)
    mixture = (latent / totals[..., None]).astype(jnp.bfloat16)
    values = jnp.einsum(
        "gihd,hdv->gihv", mixture, uv_weight, preferred_element_type=jnp.float32
    ).astype(jnp.bfloat16)
    values = values.reshape(group_count * step_count, local_heads * uv_weight.shape[2])
    partial_value = jnp.dot(values, out_weight, preferred_element_type=jnp.float32)
    result = lax.psum(partial_value.astype(jnp.bfloat16), "tp")
    return result.reshape(group_count, step_count, out_weight.shape[1])


def solution(mesh):
    placed = (
        P("pool", None, "tp"),
        P("pool", None, None),
        P("pool", "tp", None, None, None),
        P("pool", "tp", None, None, None),
        P(),
        P(),
        P("pool", "tp", None),
        P("tp", None, None),
        P("tp", None, None),
        P("tp", None),
    )
    return jax.shard_map(
        on_device, mesh=mesh, in_specs=placed, out_specs=P("pool", None, None), check_vma=False
    )
```

profile of v0, /device:TPU:9, one launch (start us, length us, event | category | flops | bytes accessed | tf_op | source)
XLA Modules:
  0.0 496.2 jit_solution(1412016093417116858)
XLA Ops:
  6.5 0.9 select_reduce_fusion.5
  8.2 0.9 copy.16
  10.3 0.8 broadcast_select_fusion.2
  15.8 8.3 %gather_fusion.2 = bf16[64,128,512]{2,1,0:T(8,128)(2,1)} fusion(bf16[44,128,512]{2,1,0:T(8,128)(2,1)} %bitcast.111, s32[1024]{0:T(1024)S(1)} %pad_clamp_fusion.2), kind=kCustom, calls=%fused_computation.4 | custom fusion | bytes 16777472 | tf_op jit(solution)/shard_map/jit(_take)/gather | solution.py:136
  24.1 7.6 %broadcast_select_fusion = bf16[8,8,128,512]{3,2,1,0:T(8,128)(2,1)} fusion(bf16[8,8,128,512]{3,2,1,0:T(8,128)(2,1)} %bitcast.109, pred[8,8]{1,0:T(8,128)(4,1)S(1)} %fusion.34), kind=kLoop, calls=%fused_computation.17 | loop fusion | flops 4194304 | bytes 16777280 | tf_op jit(solution)/shard_map/jit(_take)/select_n | solution.py:136
  31.6 5.6 %all-to-all-start = ((bf16[8,8,128,512]{3,2,1,0:T(8,128)(2,1)}), bf16[8,8,128,512]{3,2,1,0:T(8,128)(2,1)}, u32[]{:S(2)}, u32[]{:S(2)}) async-start(bf16[8,8,128,512]{3,2,1,0:T(8,128)(2,1)} %broadcast_select_fusion), calls=%async_computation | async-start | bytes 16777216 | tf_op jit(solution)/shard_map/all_to_all | solution.py:143
  37.3 0.7 gather_fusion.4
  39.3 27.9 %all_gather.7 = bf16[8,4,128,64]{3,2,1,0:T(8,128)(2,1)S(1)} all-gather(bf16[8,4,8,64]{3,2,1,0:T(8,128)(2,1)S(1)} %broadcast_select_fusion.3), channel_id=1, replica_groups=mesh['pool'=8,'tp'=16] {'tp'}, dimensions={2}, use_global_device_ids=true | all-gather | bytes 557056 | tf_op jit(solution)/shard_map/all_gather | solution.py:140
  67.5 1.2 broadcast_select_fusion.1
  68.7 61.3 %all-to-all-done = bf16[8,8,128,512]{3,2,1,0:T(8,128)(2,1)} async-done(((bf16[8,8,128,512]{3,2,1,0:T(8,128)(2,1)}), bf16[8,8,128,512]{3,2,1,0:T(8,128)(2,1)}, u32[]{:S(2)}, u32[]{:S(2)}) %all-to-all-start) | async-done | bytes 8388640 | tf_op jit(solution)/shard_map/all_to_all | solution.py:143
  130.0 5.4 %all-to-all-start.1 = ((bf16[8,8,64,128]{3,2,1,0:T(8,128)(2,1)}), bf16[8,8,64,128]{3,2,1,0:T(8,128)(2,1)S(1)}, u32[]{:S(2)}, u32[]{:S(2)}) async-start(bf16[8,8,64,128]{3,2,1,0:T(8,128)(2,1)} %broadcast_select_fusion.1), calls=%async_computation.1 | async-start | bytes 2097152 | tf_op jit(solution)/shard_map/all_to_all | solution.py:144
  135.4 14.9 %fusion.46 = f32[8,512,8,128]{1,3,2,0:T(8,128)} fusion(bf16[8,512,512,1]{2,1,3,0:T(8,128)(2,1)} %bitcast.110, bf16[8,8,128,512]{3,2,1,0:T(8,128)(2,1)} %all-to-all-done), kind=kOutput, calls=%fused_computation.112 | convolution fusion | flops 4294967296 | bytes 29360128 | tf_op jit(solution)/shard_map/sqd,scnd->sqcn/dot_general | solution.py:47
  150.4 12.5 %select_reduce_fusion = (f32[8,512]{1,0:T(8,128)S(1)}, f32[8,512,8,128]{1,3,2,0:T(8,128)}) fusion(pred[8,8,128]{2,1,0:T(8,128)(4,1)S(1)} %broadcast_compare_fusion, f32[8,512,8,128]{1,3,2,0:T(8,128)} %fusion.46, bf16[8,512,64,1]{2,1,3,0:T(8,128)(2,1)S(1)} %bitcast.112, bf16[8,8,64,128]{3,2,1,0:T(8,128)(2,1)S(1)} %all-to-all-done.1), kind=kOutput, calls=%fused_computation.10 | convolution fusion | flops 553644032 | bytes 35151872 | tf_op jit(solution)/shard_map/sqe,scen->sqcn/dot_general | solution.py:48
  162.9 61.9 %pmax.7 = f32[8,4,128]{2,1,0:T(4,128)S(1)} all-reduce(f32[8,4,128]{2,1,0:T(4,128)S(1)} %reshape.263), channel_id=1, replica_groups=mesh['pool'=8,'tp'=16] {'tp'}, use_global_device_ids=true, to_apply=%region_7.8 | all-reduce | flops 4096 | bytes 32768 | tf_op jit(solution)/shard_map/pmax | solution.py:59
  224.8 3.4 fusion.24
  228.6 13.3 %fusion.2 = f32[8,512,512,1]{2,1,3,0:T(8,128)} fusion(bf16[8,8,128,512]{3,2,1,0:T(8,128)(2,1)} %all-to-all-done, f32[8,512,8,128]{1,3,2,0:T(8,128)} %get-tuple-element.10, f32[8,512]{1,0:T(8,128)S(1)} %bitcast.118, pred[8,8,128]{2,1,0:T(8,128)(4,1)S(1)} %broadcast_compare_fusion), kind=kOutput, calls=%fused_computation.14 | convolution fusion | flops 4307550208 | bytes 33579008 | tf_op jit(solution)/shard_map/sqcn,scnd->sqd/dot_general | solution.py:65
  242.8 7.5 %fusion = f32[8,512]{1,0:T(8,128)S(1)} fusion(f32[8,512,8,128]{1,3,2,0:T(8,128)} %get-tuple-element.10, f32[8,512]{1,0:T(8,128)S(1)} %bitcast.119, pred[8,8,128]{2,1,0:T(8,128)(4,1)S(1)} %broadcast_compare_fusion), kind=kLoop, calls=%fused_computation.12 | loop fusion | flops 12578816 | bytes 16818176 | tf_op jit(solution)/shard_map/reduce_sum | solution.py:69
  250.4 57.1 %psum.22 = f32[8,4,128]{2,1,0:T(4,128)S(1)} all-reduce(f32[8,4,128]{2,1,0:T(4,128)S(1)} %reshape.265), channel_id=1, replica_groups=mesh['pool'=8,'tp'=16] {'tp'}, use_global_device_ids=true, to_apply=%region_11.13 | all-reduce | flops 4096 | bytes 32768 | tf_op jit(solution)/shard_map/psum | solution.py:70
  309.4 84.5 %all-reduce.3.cloned.1.call-done = f32[8,4,128,512]{3,2,1,0:T(8,128)} async-done(((f32[8,4,128,512]{3,2,1,0:T(8,128)}), f32[8,4,128,512]{3,2,1,0:T(8,128)}) %all-reduce.3.cloned.1.call-update) | async-done | bytes 8388624 | tf_op jit(solution)/shard_map/psum | solution.py:70
  393.9 1.1 constant_dynamic-slice_fusion.2
  396.2 7.9 %convolution_convert_fusion = bf16[32,7168]{1,0:T(8,128)(2,1)S(1)} fusion(bf16[1024,7168]{1,0:T(8,128)(2,1)} %param.21, bf16[4,8,8,128]{3,2,1,0:T(8,128)(2,1)S(1)} %bitcast.116), kind=kOutput, calls=%fused_computation.19 | convolution fusion | flops 469991424 | bytes 15204352 | tf_op jit(solution)/shard_map/dot_general | solution.py:164
  404.1 1.0 reshape.267
  405.1 82.7 %all-reduce.5.cloned.1.call-done = bf16[8,4,7168]{2,1,0:T(4,128)(2,1)} async-done(((bf16[8,4,7168]{2,1,0:T(4,128)(2,1)}), bf16[8,4,7168]{2,1,0:T(4,128)(2,1)}) %all-reduce.5.cloned.1.call-update) | async-done | bytes 458768 | tf_op jit(solution)/shard_map/psum | solution.py:165
  487.7 1.9 copy.60
  (70 shorter events, 12.4 us)
Async XLA Ops:
  6.5 2.7 copy-start
  6.5 128.9 %all-gather.2.cloned.1.call-start = ((), (), s32[]{:S(2)}) async-start(), calls=%async_computation.2 | async-start | bytes 4456448 | tf_op jit(solution)/shard_map/all_gather | solution.py:139
  31.6 5.6 %copy-start.2 = (bf16[1,1,44,64,128]{4,3,2,1,0:T(8,128)(2,1)S(1)}, bf16[1,1,44,64,128]{4,3,2,1,0:T(8,128)(2,1)}, u32[]{:S(2)}) copy-start(bf16[1,1,44,64,128]{4,3,2,1,0:T(8,128)(2,1)} %param.15) | copy-start | bytes 2162692
  31.6 7.0 %copy-start.4 = (bf16[8,4,576]{2,1,0:T(4,128)(2,1)S(1)}, bf16[8,4,576]{2,1,0:T(4,128)(2,1)}, u32[]{:S(2)}) copy-start(bf16[8,4,576]{2,1,0:T(4,128)(2,1)} %param.13) | copy-start | bytes 110596
  31.6 98.4 %all-to-all-start = ((bf16[8,8,128,512]{3,2,1,0:T(8,128)(2,1)}), bf16[8,8,128,512]{3,2,1,0:T(8,128)(2,1)}, u32[]{:S(2)}, u32[]{:S(2)}) async-start(bf16[8,8,128,512]{3,2,1,0:T(8,128)(2,1)} %broadcast_select_fusion), calls=%async_computation | async-start | bytes 16777216 | tf_op jit(solution)/shard_map/all_to_all | solution.py:143
  130.0 20.4 %all-to-all-start.1 = ((bf16[8,8,64,128]{3,2,1,0:T(8,128)(2,1)}), bf16[8,8,64,128]{3,2,1,0:T(8,128)(2,1)S(1)}, u32[]{:S(2)}, u32[]{:S(2)}) async-start(bf16[8,8,64,128]{3,2,1,0:T(8,128)(2,1)} %broadcast_select_fusion.1), calls=%async_computation.1 | async-start | bytes 2097152 | tf_op jit(solution)/shard_map/all_to_all | solution.py:144
  135.4 258.4 %all-reduce.3.cloned.1.call-start = ((), (), s32[]{:S(2)}) async-start(), calls=%async_computation.3 | async-start | bytes 16777216 | tf_op jit(solution)/shard_map/psum | solution.py:70
  242.0 245.7 %all-reduce.5.cloned.1.call-start = ((), (), s32[]{:S(2)}) async-start(), calls=%async_computation.4 | async-start | bytes 917504 | tf_op jit(solution)/shard_map/psum | solution.py:165
  242.8 153.0 %copy-start.3 = (bf16[8,512,128]{2,1,0:T(8,128)(2,1)S(1)}, bf16[8,512,128]{2,1,0:T(8,128)(2,1)}, u32[]{:S(2)}) copy-start(bf16[8,512,128]{2,1,0:T(8,128)(2,1)} %param.20) | copy-start | bytes 3145732
  396.2 93.5 %copy-start.1 = (bf16[8,128,512]{2,1,0:T(8,128)(2,1)S(1)}, bf16[8,128,512]{2,1,0:T(8,128)(2,1)}, u32[]{:S(2)}) copy-start(bf16[8,128,512]{2,1,0:T(8,128)(2,1)} %param.19) | copy-start | bytes 3145732
Sparse Core Ops, SparseCore 0:
  11.2 64.2 all-gather.1
  242.1 151.6 all-reduce.2
  405.2 82.4 all-reduce.4
where the time goes:
time: 498 us; the launch traced here: 496 us
  waiting for transfers between devices  229 us (46%)
  blocking collectives  147 us (30%)
  matrix products  54.4 us (11%)
  other arithmetic  22.5 us (5%)
  local copies, waits for them, and re-layouts  19.4 us (4%)
  between operations  13.4 us (3%)
  starting transfers between devices  11.1 us (2%)
    psum x1, waiting for transfers between devices, attend(): latent, totals = lax.psum((latent, totals), 'tp')  84.5 us
    psum x1, waiting for transfers between devices, on_device(): result = lax.psum(partial_value.astype(jnp.bfloat16), 'tp')  82.7 us
    pmax x1, blocking collectives, attend(): maxima = jnp.maximum(lax.pmax(cache_max, 'tp'), fresh_peak)  61.9 us
    all_to_all x1, waiting for transfers between devices, on_device(): lax.all_to_all(latent_out, 'pool', split_axis=0, concat_axis=0, tiled=True)  61.3 us
    psum x1, blocking collectives, attend(): latent, totals = lax.psum((latent, totals), 'tp')  57.1 us
    all_gather x1, blocking collectives, on_device(): lax.all_gather(mine_rope, 'tp', axis=2, tiled=True)  27.9 us
    dot_general x1, matrix products, attend(): jnp.einsum('sqd,scnd->sqcn', flat_latent, latents, preferred_element_type...  14.9 us
    dot_general x1, matrix products, attend(): jnp.einsum('sqcn,scnd->sqd', weights.astype(jnp.bfloat16), latents, prefe...  13.3 us
  transfers between devices with their start and end apart: 5, of which 3 were waited for; matrix products, arithmetic and copies ran while one was open for 10% of the time, Pallas kernels for 0%

commit v1 on v0

v1 whole, which is shorter than its diff:
```python
import jax
import jax.numpy as jnp
from jax import lax
from jax.experimental import pallas as pl
from jax.experimental.pallas import tpu as pltpu
from jax.sharding import PartitionSpec as P

MESH = pl.DeviceIdType.MESH
F32 = jnp.float32
BF16 = jnp.bfloat16
MASKED = -1e30

POOL = 8
SIDE = 4
TP = 16
SEQ = 8
STEPS = 4
HEADS = 8
NOPE = 128
ROPE = 64
RANK = 512
BLOCKS = 44
ROWS = 128
SLOTS = 8
KEYS = SLOTS * ROWS
SHARD = HEADS * STEPS
PACK = SHARD * 4 + SHARD // 2
WIDTH = 7168
CHUNK = 896
SCALE = (NOPE + ROPE) ** -0.5


def iota(shape, dim):
    return lax.broadcasted_iota(jnp.int32, shape, dim)


def dot(a, b):
    return jnp.dot(a, b, preferred_element_type=F32)


def dot_nt(a, b):
    return lax.dot_general(a, b, (((1,), (1,)), ((), ())), preferred_element_type=F32)


def two_columns(first, second):
    lane = iota((first.shape[0], 128), 1)
    return jnp.where(lane == 0, first, jnp.where(lane == 1, second, 0.0))


def merge(parts):
    top = parts[0][1]
    for part in parts[1:]:
        top = jnp.maximum(top, part[1])
    sums, totals = 0.0, 0.0
    for part in parts:
        factor = jnp.exp(part[1] - top)
        sums = sums + factor * part[0].astype(F32)
        totals = totals + factor * part[2]
    return sums, top, totals


def kernel(
    owner,
    lengths,
    packing,
    queries_hbm,
    fresh_hbm,
    latent_hbm,
    rope_hbm,
    uk_hbm,
    uv_hbm,
    out_weight_hbm,
    out_ref,
    queries,
    fresh,
    latents,
    ropes,
    uk,
    uv,
    out_weight,
    wide,
    absorbed,
    outgoing,
    gathered,
    keys,
    rope_keys,
    sums1,
    stats1,
    sums1_in,
    stats1_in,
    sums2,
    stats2,
    sums2_in,
    stats2_in,
    turned,
    sums3,
    stats3,
    sums3_in,
    stats3_in,
    fresh_sums,
    fresh_stats,
    part_out,
    part_in,
    local_sem,
    a2a_send,
    a2a_recv,
    ag1_send,
    ag1_recv,
    ag2_send,
    ag2_recv,
    rs1_send,
    rs1_recv,
    rs1s_send,
    rs1s_recv,
    rs2_send,
    rs2_recv,
    rs2s_send,
    rs2s_recv,
    ret_send,
    ret_recv,
    rets_send,
    rets_recv,
    fin_send,
    fin_recv,
    all_send,
    all_recv,
):
    pool = lax.axis_index("pool")
    tp = lax.axis_index("tp")
    z, x = tp // SIDE, tp % SIDE

    def load(index, source, target):
        return pltpu.make_async_copy(source, target, local_sem.at[index])

    loads = [
        load(0, queries_hbm, queries),
        load(1, uk_hbm, uk),
        load(2, fresh_hbm, fresh),
        load(3, latent_hbm, latents),
        load(4, rope_hbm, ropes),
    ]
    for h in range(HEADS):
        loads.append(load(5 + h, uv_hbm.at[h], uv.at[:, h * 128 : (h + 1) * 128]))
    loads.append(load(5 + HEADS, out_weight_hbm, out_weight))
    for copy in loads:
        copy.start()

    barrier = pltpu.get_barrier_semaphore()
    for j in range(1, POOL):
        pl.semaphore_signal(
            barrier, inc=1, device_id=((pool + j) % POOL, tp), device_id_type=MESH
        )
    for j in range(1, TP):
        pl.semaphore_signal(barrier, inc=1, device_id=(pool, (tp + j) % TP), device_id_type=MESH)

    def slot_of(s, g):
        slot = jnp.int32(0)
        for k in range(1, SEQ):
            slot = jnp.where(owner[s, k] == g, k, slot)
        return slot

    slots = [slot_of((pool + POOL - d) % POOL, pool) for d in range(SEQ)]

    def slot_vector(which):
        vector = jnp.zeros(which.shape, jnp.int32)
        for d in range(SEQ):
            vector = jnp.where(which == d, slots[d], vector)
        return vector

    wide[...] = jnp.zeros_like(wide)
    row, lane = iota((ROPE, 128), 0), iota((ROPE, 128), 1)
    unit = jnp.where((lane & (ROPE - 1)) == row, 1.0, 0.0).astype(BF16)
    for h in range(HEADS):
        start = h * (NOPE + ROPE)
        wide[start + NOPE : start + NOPE + ROPE, RANK:] = unit
    loads[1].wait()
    for h in range(HEADS):
        start = h * (NOPE + ROPE)
        wide[start : start + NOPE, :RANK] = uk[h]
    count = SEQ * SHARD
    row, col = iota((count, SEQ * STEPS), 0), iota((count, SEQ * STEPS), 1)
    pick = ((col >> 2) == slot_vector(row >> 5)) & ((col & 3) == (row & 3))
    loads[0].wait()
    spread = dot(jnp.where(pick, 1.0, 0.0).astype(BF16), queries[...])
    row, lane = iota(spread.shape, 0), iota(spread.shape, 1)
    first = ((row >> 2) & (HEADS - 1)) * (NOPE + ROPE)
    spread = jnp.where((lane >= first) & (lane < first + NOPE + ROPE), spread, 0.0)
    absorbed[...] = dot(spread.astype(BF16), wide[...]).astype(BF16)

    def place(par):
        return z + par * (x - z), x + par * (z - x)

    def minor_peer(par, j):
        major, minor = place(par)
        to = (minor + j) % SIDE
        return to, (pool, (1 - par) * (z * SIDE + to) + par * (to * SIDE + x))

    def major_peer(par, j):
        major, minor = place(par)
        to = (major + j) % SIDE
        return to, (pool, (1 - par) * (to * SIDE + x) + par * (z * SIDE + to))

    def remote(source, target, send, recv, device):
        return pltpu.make_async_remote_copy(
            src_ref=source,
            dst_ref=target,
            send_sem=send,
            recv_sem=recv,
            device_id=device,
            device_id_type=MESH,
        )

    def a2a(d):
        major, minor = place(d % 2)
        return remote(
            outgoing.at[d],
            gathered.at[d, major * SIDE + minor],
            a2a_send.at[d],
            a2a_recv.at[d],
            ((pool + POOL - d) % POOL, tp),
        )

    def ag1(d, j):
        major, minor = place(d % 2)
        piece = gathered.at[d, major * SIDE + minor]
        return remote(
            piece, piece, ag1_send.at[d, j], ag1_recv.at[d, j], minor_peer(d % 2, j + 1)[1]
        )

    def ag2(d, j):
        major, minor = place(d % 2)
        piece = gathered.at[d, pl.ds(major * SIDE, SIDE)]
        return remote(
            piece, piece, ag2_send.at[d, j], ag2_recv.at[d, j], major_peer(d % 2, j + 1)[1]
        )

    def rs1(d, j):
        to, device = major_peer(d % 2, j + 1)
        return (
            remote(
                sums1.at[d, pl.ds(to * SIDE, SIDE)],
                sums1_in.at[d, j],
                rs1_send.at[d, j],
                rs1_recv.at[d, j],
                device,
            ),
            remote(
                stats1.at[d, to],
                stats1_in.at[d, j],
                rs1s_send.at[d, j],
                rs1s_recv.at[d, j],
                device,
            ),
        )

    def rs2(d, j):
        to, device = minor_peer(d % 2, j + 1)
        return (
            remote(
                sums2.at[d, to],
                sums2_in.at[d, j],
                rs2_send.at[d, j],
                rs2_recv.at[d, j],
                device,
            ),
            remote(
                stats2.at[d],
                stats2_in.at[d, j],
                rs2s_send.at[d, j],
                rs2s_recv.at[d, j],
                device,
            ),
        )

    def back(d):
        device = ((pool + d) % POOL, tp)
        return (
            remote(sums3.at[d], sums3_in.at[d], ret_send.at[d], ret_recv.at[d], device),
            remote(stats3.at[d], stats3_in.at[d], rets_send.at[d], rets_recv.at[d], device),
        )

    def packed(d):
        rows = slice(d * SHARD, (d + 1) * SHARD)
        chunks = [absorbed[rows, c * 128 : (c + 1) * 128] for c in range(4)]
        rotary = absorbed[rows, RANK:]
        half = SHARD // 2
        lane = iota((half, 128), 1)
        chunks.append(jnp.where(lane < ROPE, rotary[:half], rotary[half:]))
        return jnp.concatenate(chunks, axis=0)

    major, minor = place(0)
    gathered[0, major * SIDE + minor] = packed(0)
    for d in range(1, SEQ):
        outgoing[d] = packed(d)
    pl.semaphore_wait(barrier, POOL - 1 + TP - 1)
    for d in range(1, SEQ):
        a2a(d).start()

    def gather(i, carry):
        @pl.when(i < SEQ)
        def _():
            @pl.when(i > 0)
            def _():
                a2a(i).wait_recv()

            for j in range(SIDE - 1):
                ag1(i, j).start()

        @pl.when(i > 0)
        def _():
            for j in range(SIDE - 1):
                ag1(i - 1, j).wait_recv()
            for j in range(SIDE - 1):
                ag2(i - 1, j).start()

        return carry

    lax.fori_loop(0, SEQ + 1, gather, 0)

    loads[2].wait()
    row, col = iota((SEQ * STEPS, SEQ * STEPS), 0), iota((SEQ * STEPS, SEQ * STEPS), 1)
    pick = ((col >> 2) == slot_vector(row >> 2)) & ((col & 3) == (row & 3))
    ordered = dot(jnp.where(pick, 1.0, 0.0).astype(BF16), fresh[...]).astype(BF16)
    scores = dot_nt(absorbed[...], ordered) * SCALE
    row, col = iota(scores.shape, 0), iota(scores.shape, 1)
    causal = ((col >> 2) == (row >> 5)) & ((col & 3) <= (row & 3))
    top = jnp.max(jnp.where(causal, scores, MASKED), axis=1, keepdims=True)
    weights = jnp.where(causal, jnp.exp(scores - top), 0.0)
    high = weights.astype(BF16)
    low = (weights - high.astype(F32)).astype(BF16)
    fresh_sums[...] = dot(high, ordered[:, :RANK]) + dot(low, ordered[:, :RANK])
    fresh_stats[...] = two_columns(top, jnp.sum(weights, axis=1, keepdims=True))

    rope_keys[...] = jnp.zeros_like(rope_keys)
    loads[3].wait()
    loads[4].wait()

    def attend(d):
        target = (pool + d) % POOL
        slot = slot_of(pool, target)
        length = lengths[pool, slot]
        start, running = jnp.int32(0), jnp.int32(0)
        for k in range(SEQ):
            other = packing[k]
            start = jnp.where(other == slot, running, start)
            stored = (lengths[pool, other] + ROWS - 1) // ROWS - tp + TP - 1
            running = running + stored // TP
        for c in range(SLOTS):
            index = jnp.minimum(start + c, BLOCKS - 1)
            keys[c * ROWS : (c + 1) * ROWS, :] = latents[index]
            rope_keys[ROPE : 2 * ROPE, c * ROWS : (c + 1) * ROWS] = ropes[index]

        def half(i, carry):
            shards = TP // 2
            rows = shards * SHARD
            part = gathered[d, pl.ds(i * shards, shards)]
            latent_query = jnp.concatenate(
                [part[:, c * SHARD : (c + 1) * SHARD].reshape(rows, 128) for c in range(4)], axis=1
            )
            rope_query = part[:, 4 * SHARD :].reshape(rows // 2, 128)
            upper = dot(rope_query, rope_keys[ROPE : 3 * ROPE]).reshape(shards, SHARD // 2, KEYS)
            lower = dot(rope_query, rope_keys[: 2 * ROPE]).reshape(shards, SHARD // 2, KEYS)
            rotary = jnp.concatenate([upper, lower], axis=1).reshape(rows, KEYS)
            scores = (dot_nt(latent_query, keys[...]) + rotary) * SCALE
            lane = iota((1, KEYS), 1)
            position = ROWS * (tp + TP * (lane >> 7)) + (lane & (ROWS - 1))
            usable = position < length
            top = jnp.max(jnp.where(usable, scores, MASKED), axis=1, keepdims=True)
            weights = jnp.where(usable, jnp.exp(scores - top), 0.0)
            total = jnp.sum(weights, axis=1, keepdims=True)
            sums = dot(weights.astype(BF16), keys[...])
            sums1[d, pl.ds(i * shards, shards)] = sums.astype(BF16).reshape(shards, SHARD, RANK)
            columns = two_columns(top, total)
            for part_index in range(2):
                block = columns[part_index * 128 : (part_index + 1) * 128]
                stats1[d, i * 2 + part_index] = block.T[:8]
            return carry

        lax.fori_loop(0, 2, half, 0)

    def columns_of(first, others):
        rows = [first] + [others[j] for j in range(SIDE - 1)]
        rows.append(jnp.zeros((128 - 8 * SIDE, 128), F32))
        return jnp.concatenate(rows, axis=0).T

    def merge1(d):
        major, minor = place(d % 2)
        columns = columns_of(stats1[d, major], [stats1_in[d, j] for j in range(SIDE - 1)])
        pieces = [sums1[d, pl.ds(major * SIDE, SIDE)]]
        pieces += [sums1_in[d, j] for j in range(SIDE - 1)]
        parts = []
        for j, piece in enumerate(pieces):
            parts.append(
                (
                    piece.reshape(SIDE * SHARD, RANK),
                    columns[:, 8 * j : 8 * j + 1],
                    columns[:, 8 * j + 1 : 8 * j + 2],
                )
            )
        sums, top, total = merge(parts)
        sums2[d] = sums.astype(BF16).reshape(SIDE, SHARD, RANK)
        stats2[d] = two_columns(top, total).T[:8]

    def merge2(d):
        major, minor = place(d % 2)
        columns = columns_of(stats2[d], [stats2_in[d, j] for j in range(SIDE - 1)])
        turned[...] = columns.reshape(SIDE, SHARD, 128)
        columns = turned[minor]
        pieces = [sums2[d, minor]] + [sums2_in[d, j] for j in range(SIDE - 1)]
        parts = []
        for j, piece in enumerate(pieces):
            parts.append((piece, columns[:, 8 * j : 8 * j + 1], columns[:, 8 * j + 1 : 8 * j + 2]))
        sums, top, total = merge(parts)
        return sums.astype(BF16), two_columns(top, total)

    def work(i, carry):
        @pl.when(i < SEQ)
        def _():
            for j in range(SIDE - 1):
                ag2(i, j).wait_recv()
            attend(i)
            for j in range(SIDE - 1):
                for copy in rs1(i, j):
                    copy.start()

        @pl.when((i >= 1) & (i < SEQ + 1))
        def _():
            d = i - 1
            for j in range(SIDE - 1):
                for copy in rs1(d, j):
                    copy.wait_recv()
            merge1(d)
            for j in range(SIDE - 1):
                for copy in rs2(d, j):
                    copy.start()

        @pl.when(i >= 2)
        def _():
            d = i - 2
            for j in range(SIDE - 1):
                for copy in rs2(d, j):
                    copy.wait_recv()
            sums, stats = merge2(d)

            @pl.when(d == 0)
            def _():
                sums3_in[0] = sums
                stats3_in[0] = stats

            @pl.when(d > 0)
            def _():
                sums3[d] = sums
                stats3[d] = stats
                for copy in back(d):
                    copy.start()

        return carry

    lax.fori_loop(0, SEQ + 2, work, 0)

    for d in range(1, SEQ):
        for copy in back(d):
            copy.wait_recv()
    columns = stats3_in[...].reshape(count, 128)
    fresh_columns = fresh_stats[...]
    sums, top, total = merge(
        [
            (sums3_in[...].reshape(count, RANK), columns[:, 0:1], columns[:, 1:2]),
            (fresh_sums[...], fresh_columns[:, 0:1], fresh_columns[:, 1:2]),
        ]
    )
    mixture = (sums / total).astype(BF16)
    for copy in loads[5 : 5 + HEADS]:
        copy.wait()
    values = dot(mixture, uv[...])
    row, lane = iota(values.shape, 0), iota(values.shape, 1)
    values = jnp.where((lane >> 7) == ((row >> 2) & (HEADS - 1)), values, 0.0).astype(BF16)
    row, col = iota((SEQ * STEPS, count), 0), iota((SEQ * STEPS, count), 1)
    pick = ((row >> 2) == slot_vector(col >> 5)) & ((row & 3) == (col & 3))
    values = dot(jnp.where(pick, 1.0, 0.0).astype(BF16), values).astype(BF16)

    def scatter(to):
        return remote(
            part_out.at[to], part_in.at[tp], fin_send.at[to], fin_recv.at[tp], (pool, to)
        )

    def arrive(source):
        return remote(
            part_out.at[source],
            part_in.at[source],
            fin_send.at[source],
            fin_recv.at[source],
            (pool, source),
        )

    half = TP // 2
    loads[5 + HEADS].wait()

    def project(c, carry):
        cols = pl.ds(pl.multiple_of(c * CHUNK, 128), CHUNK)
        part = dot(values, out_weight[:, cols]).astype(BF16)
        for r in range(2):
            to = r * half + c
            part_out[to] = part[r * 16 : (r + 1) * 16]

            @pl.when(to != tp)
            def _():
                scatter(to).start()

        return carry

    lax.fori_loop(0, half, project, 0)
    for j in range(1, TP):
        arrive((tp + j) % TP).wait_recv()
    total = part_out[tp].astype(F32)
    for j in range(1, TP):
        total = total + part_in[(tp + j) % TP].astype(F32)

    def chunk_of(index):
        rows = pl.ds(pl.multiple_of(index // half * 16, 16), 16)
        return out_ref.at[rows, pl.ds(pl.multiple_of(index % half * CHUNK, 128), CHUNK)]

    mine = chunk_of(tp)
    mine[...] = total.astype(BF16)

    def spread_out(to):
        return remote(mine, mine, all_send.at[to], all_recv.at[tp], (pool, to))

    def collect(source):
        piece = chunk_of(source)
        return remote(piece, piece, all_send.at[source], all_recv.at[source], (pool, source))

    for j in range(1, TP):
        spread_out((tp + j) % TP).start()
    for j in range(1, TP):
        collect((tp + j) % TP).wait_recv()

    for j in range(1, TP):
        scatter((tp + j) % TP).wait_send()
        spread_out((tp + j) % TP).wait_send()

    def drain(d, carry):
        for j in range(SIDE - 1):
            ag1(d, j).wait_send()
            ag2(d, j).wait_send()
            for copy in rs1(d, j) + rs2(d, j):
                copy.wait_send()

        @pl.when(d > 0)
        def _():
            a2a(d).wait_send()
            for copy in back(d):
                copy.wait_send()

        return carry

    lax.fori_loop(0, SEQ, drain, 0)


def on_device(
    queries,
    new_rows,
    prefill_latent,
    prefill_rope,
    lengths,
    owner,
    pack_order,
    uk_weight,
    uv_weight,
    out_weight,
):
    rows = SEQ * STEPS
    fresh = jnp.pad(new_rows.reshape(rows, RANK + ROPE), ((0, 0), (0, 128 - ROPE)))
    dma = pltpu.SemaphoreType.DMA
    anywhere = pl.BlockSpec(memory_space=pl.ANY)
    scalars = pl.BlockSpec(memory_space=pltpu.SMEM)
    out = pl.pallas_call(
        kernel,
        out_shape=jax.ShapeDtypeStruct((rows, WIDTH), BF16),
        in_specs=[scalars] * 3 + [anywhere] * 7,
        out_specs=pl.BlockSpec(memory_space=pltpu.VMEM),
        scratch_shapes=[
            pltpu.VMEM((rows, HEADS * (NOPE + ROPE)), BF16),
            pltpu.VMEM((rows, RANK + 128), BF16),
            pltpu.VMEM((BLOCKS, ROWS, RANK), BF16),
            pltpu.VMEM((BLOCKS, ROPE, ROWS), BF16),
            pltpu.VMEM((HEADS, NOPE, RANK), BF16),
            pltpu.VMEM((RANK, HEADS * 128), BF16),
            pltpu.VMEM((HEADS * 128, WIDTH), BF16),
            pltpu.VMEM((HEADS * (NOPE + ROPE), RANK + 128), BF16),
            pltpu.VMEM((SEQ * SHARD, RANK + 128), BF16),
            pltpu.VMEM((SEQ, PACK, 128), BF16),
            pltpu.VMEM((SEQ, TP, PACK, 128), BF16),
            pltpu.VMEM((KEYS, RANK), BF16),
            pltpu.VMEM((3 * ROPE, KEYS), BF16),
            pltpu.VMEM((SEQ, TP, SHARD, RANK), BF16),
            pltpu.VMEM((SEQ, SIDE, 8, 128), F32),
            pltpu.VMEM((SEQ, SIDE - 1, SIDE, SHARD, RANK), BF16),
            pltpu.VMEM((SEQ, SIDE - 1, 8, 128), F32),
            pltpu.VMEM((SEQ, SIDE, SHARD, RANK), BF16),
            pltpu.VMEM((SEQ, 8, 128), F32),
            pltpu.VMEM((SEQ, SIDE - 1, SHARD, RANK), BF16),
            pltpu.VMEM((SEQ, SIDE - 1, 8, 128), F32),
            pltpu.VMEM((SIDE, SHARD, 128), F32),
            pltpu.VMEM((SEQ, SHARD, RANK), BF16),
            pltpu.VMEM((SEQ, SHARD, 128), F32),
            pltpu.VMEM((SEQ, SHARD, RANK), BF16),
            pltpu.VMEM((SEQ, SHARD, 128), F32),
            pltpu.VMEM((SEQ * SHARD, RANK), F32),
            pltpu.VMEM((SEQ * SHARD, 128), F32),
            pltpu.VMEM((TP, 16, CHUNK), BF16),
            pltpu.VMEM((TP, 16, CHUNK), BF16),
            dma((6 + HEADS,)),
        ]
        + [dma((SEQ,))] * 2
        + [dma((SEQ, SIDE - 1))] * 12
        + [dma((SEQ,))] * 4
        + [dma((TP,))] * 4,
        compiler_params=pltpu.CompilerParams(
            collective_id=0, has_side_effects=True, vmem_limit_bytes=60 << 20
        ),
    )(
        owner,
        lengths,
        pack_order.reshape(SEQ),
        queries.reshape(rows, HEADS * (NOPE + ROPE)),
        fresh,
        prefill_latent.reshape(BLOCKS, ROWS, RANK),
        prefill_rope.reshape(BLOCKS, ROPE, ROWS),
        uk_weight,
        uv_weight,
        out_weight,
    )
    return out.reshape(SEQ, STEPS, WIDTH)


def solution(mesh):
    placed = (
        P("pool", None, "tp"),
        P("pool", None, None),
        P("pool", "tp", None, None, None),
        P("pool", "tp", None, None, None),
        P(),
        P(),
        P("pool", "tp", None),
        P("tp", None, None),
        P("tp", None, None),
        P("tp", None),
    )
    return jax.shard_map(
        on_device, mesh=mesh, in_specs=placed, out_specs=P("pool", None, None), check_vma=False
    )
```

time: 498 us -> 126 us (0.25)
  waiting for transfers between devices: 229 us -> 0 us
  blocking collectives: 147 us -> 0 us
  Pallas kernels: 0 us -> 121 us
  matrix products: 54.4 us -> 0 us
  other arithmetic: 22.5 us -> 0 us
  local copies, waits for them, and re-layouts: 19.4 us -> 4.93 us
  between operations: 13.4 us -> 0.01 us
  starting transfers between devices: 11.1 us -> 0 us
    psum x2 -> x0, waiting for transfers between devices: 167 us -> none  [the longest x1 84.5 us: attend(): latent, totals = lax.psum((latent, totals), 'tp')]
    pallas_call x0 -> x1, Pallas kernels: none -> 121 us  [on_device(): pl.pallas_call(kernel, out_shape=jax.ShapeDtypeStruct((rows, WIDTH), BF16...]
    pmax x1 -> x0, blocking collectives: 61.9 us -> none  [attend(): maxima = jnp.maximum(lax.pmax(cache_max, 'tp'), fresh_peak)]
    all_to_all x2 -> x0, waiting for transfers between devices: 61.3 us -> none  [the longest x1 61.3 us: on_device(): lax.all_to_all(latent_out, 'pool', split_axis=0, concat_axis=0, tiled=True)]
    psum x1 -> x0, blocking collectives: 57.1 us -> none  [attend(): latent, totals = lax.psum((latent, totals), 'tp')]
    dot_general x11 -> x0, matrix products: 54.4 us -> none  [the longest x1 14.9 us: attend(): jnp.einsum('sqd,scnd->sqcn', flat_latent, latents, preferred_element_type...]
    all_gather x1 -> x0, blocking collectives: 27.9 us -> none  [on_device(): lax.all_gather(mine_rope, 'tp', axis=2, tiled=True)]
    gather x9 -> x0, local copies, waits for them, and re-layouts: 13.1 us -> none  [the longest x1 8.29 us: on_device(): latent_out = jnp.take(prefill_latent[0, 0], block_index, axis=0)]
  transfers between devices with their start and end apart: 5 -> 0, of which waited for: 3 -> 0; matrix products, arithmetic and copies ran while one was open for 10% -> 0% of each run, Pallas kernels for 0% -> 0%
where the time goes in v1:
time: 126 us
  Pallas kernels  121 us (96%)
  local copies, waits for them, and re-layouts  4.93 us (4%)
    pallas_call x1, Pallas kernels, on_device(): pl.pallas_call(kernel, out_shape=jax.ShapeDtypeStruct((rows, WIDTH), BF16...  121 us

profile of v1, /device:TPU:9, one launch (start us, length us, event | category | flops | bytes accessed | tf_op | source)
XLA Modules:
  0.0 125.8 jit_solution(6626737205307843957)
XLA Ops:
  0.0 0.8 reshape.20
  0.8 0.6 pad.4.fresh_hbm
  1.4 1.6 %reshape.19.queries_hbm = bf16[32,1536]{1,0:T(8,128)(2,1)} reshape(bf16[8,4,1536]{2,1,0:T(4,128)(2,1)} %param.10) | data formatting | bytes 196608 | tf_op jit(solution)/shard_map/reshape | solution.py:626
  3.0 120.9 %shard_map.100 = bf16[32,7168]{1,0:T(8,128)(2,1)} custom-call(s32[8,8]{1,0:T(8,128)} %owner.1, s32[8,8]{1,0:T(8,128)} %lengths.1, s32[8]{0:T(128)} %bitcast.5, bf16[32,1536]{1,0:T(8,128)(2,1)} %reshape.19.queries_hbm, bf16[32,640]{1,0:T(8,128)(2,1)} %pad.4.fresh_hbm, bf16[44,128,512]{2,1,0:T(8,128)(2,1)} %bitcast.3, bf16[44,64,128]{2,1,0:T(8,128)(2,1)} %bitcast.4, ...), custom_call_target="tpu_custom_call" | custom-call | tf_op jit(solution)/shard_map/pallas_call | solution.py:577
  123.9 2.0 %reshape.23 = bf16[8,4,7168]{2,1,0:T(4,128)(2,1)} reshape(bf16[32,7168]{1,0:T(8,128)(2,1)} %shard_map.100) | data formatting | bytes 917504 | tf_op jit(solution)/shard_map/reshape | solution.py:634

commit v2 on v1

--- a/solution.py
+++ b/solution.py
@@ -28,6 +28,9 @@
 WIDTH = 7168
 CHUNK = 896
 SCALE = (NOPE + ROPE) ** -0.5
+PARTS = 4
+AHEAD1, AHEAD2, AHEAD3 = 5, 3, 1
+BEHIND0, BEHIND1, BEHIND2 = 1, 2, 3
 
 
 def iota(shape, dim):
@@ -73,6 +76,8 @@
     out_ref,
     queries,
     fresh,
+    flat_queries,
+    flat_fresh,
     latents,
     ropes,
     uk,
@@ -86,6 +91,8 @@
     rope_keys,
     sums1,
     stats1,
+    sums0_in,
+    stats0_in,
     sums1_in,
     stats1_in,
     sums2,
@@ -93,12 +100,9 @@
     sums2_in,
     stats2_in,
     turned,
-    sums3,
-    stats3,
-    sums3_in,
-    stats3_in,
     fresh_sums,
     fresh_stats,
+    mixture,
     part_out,
     part_in,
     local_sem,
@@ -106,20 +110,22 @@
     a2a_recv,
     ag1_send,
     ag1_recv,
+    ret_send,
+    ret_recv,
+    rets_send,
+    rets_recv,
     ag2_send,
     ag2_recv,
+    ag3_send,
+    ag3_recv,
+    rs0_send,
+    rs0_recv,
+    rs0s_send,
+    rs0s_recv,
     rs1_send,
     rs1_recv,
     rs1s_send,
     rs1s_recv,
-    rs2_send,
-    rs2_recv,
-    rs2s_send,
-    rs2s_recv,
-    ret_send,
-    ret_recv,
-    rets_send,
-    rets_recv,
     fin_send,
     fin_recv,
     all_send,
@@ -129,6 +135,29 @@
     tp = lax.axis_index("tp")
     z, x = tp // SIDE, tp % SIDE
 
+    def place(par):
+        return z + par * (x - z), x + par * (z - x)
+
+    def minor_peer(par, j):
+        major, minor = place(par)
+        to = (minor + j) % SIDE
+        return to, (pool, (1 - par) * (z * SIDE + to) + par * (to * SIDE + x))
+
+    def major_peer(par, j):
+        major, minor = place(par)
+        to = (major + j) % SIDE
+        return to, (pool, (1 - par) * (to * SIDE + x) + par * (z * SIDE + to))
+
+    def remote(source, target, send, recv, device):
+        return pltpu.make_async_remote_copy(
+            src_ref=source,
+            dst_ref=target,
+            send_sem=send,
+            recv_sem=recv,
+            device_id=device,
+            device_id_type=MESH,
+        )
+
     def load(index, source, target):
         return pltpu.make_async_copy(source, target, local_sem.at[index])
 
@@ -136,20 +165,29 @@
         load(0, queries_hbm, queries),
         load(1, uk_hbm, uk),
         load(2, fresh_hbm, fresh),
-        load(3, latent_hbm, latents),
-        load(4, rope_hbm, ropes),
     ]
-    for h in range(HEADS):
-        loads.append(load(5 + h, uv_hbm.at[h], uv.at[:, h * 128 : (h + 1) * 128]))
-    loads.append(load(5 + HEADS, out_weight_hbm, out_weight))
     for copy in loads:
         copy.start()
 
+    def cache_loads(part):
+        piece = pl.ds(part * (BLOCKS // PARTS), BLOCKS // PARTS)
+        return (
+            load(3 + part, latent_hbm.at[piece], latents.at[piece]),
+            load(3 + PARTS + part, rope_hbm.at[piece], ropes.at[piece]),
+        )
+
+    def weight_loads(h):
+        piece = pl.ds(pl.multiple_of(h * 128, 128), 128)
+        return (
+            load(3 + 2 * PARTS + h, uv_hbm.at[h], uv.at[:, piece]),
+            load(3 + 2 * PARTS + HEADS + h, out_weight_hbm.at[piece], out_weight.at[piece]),
+        )
+
     barrier = pltpu.get_barrier_semaphore()
-    for j in range(1, POOL):
-        pl.semaphore_signal(
-            barrier, inc=1, device_id=((pool + j) % POOL, tp), device_id_type=MESH
-        )
+    for d in range(1, POOL):
+        for j in range(SIDE):
+            device = ((pool + d) % POOL, minor_peer(d % 2, j)[1][1])
+            pl.semaphore_signal(barrier, inc=1, device_id=device, device_id_type=MESH)
     for j in range(1, TP):
         pl.semaphore_signal(barrier, inc=1, device_id=(pool, (tp + j) % TP), device_id_type=MESH)
 
@@ -181,34 +219,13 @@
     row, col = iota((count, SEQ * STEPS), 0), iota((count, SEQ * STEPS), 1)
     pick = ((col >> 2) == slot_vector(row >> 5)) & ((col & 3) == (row & 3))
     loads[0].wait()
-    spread = dot(jnp.where(pick, 1.0, 0.0).astype(BF16), queries[...])
+    for k in range(SEQ):
+        flat_queries[k * STEPS : (k + 1) * STEPS] = queries[k].astype(F32)
+    spread = dot(jnp.where(pick, 1.0, 0.0).astype(BF16), flat_queries[...].astype(BF16))
     row, lane = iota(spread.shape, 0), iota(spread.shape, 1)
     first = ((row >> 2) & (HEADS - 1)) * (NOPE + ROPE)
     spread = jnp.where((lane >= first) & (lane < first + NOPE + ROPE), spread, 0.0)
     absorbed[...] = dot(spread.astype(BF16), wide[...]).astype(BF16)
-
-    def place(par):
-        return z + par * (x - z), x + par * (z - x)
-
-    def minor_peer(par, j):
-        major, minor = place(par)
-        to = (minor + j) % SIDE
-        return to, (pool, (1 - par) * (z * SIDE + to) + par * (to * SIDE + x))
-
-    def major_peer(par, j):
-        major, minor = place(par)
-        to = (major + j) % SIDE
-        return to, (pool, (1 - par) * (to * SIDE + x) + par * (z * SIDE + to))
-
-    def remote(source, target, send, recv, device):
-        return pltpu.make_async_remote_copy(
-            src_ref=source,
-            dst_ref=target,
-            send_sem=send,
-            recv_sem=recv,
-            device_id=device,
-            device_id_type=MESH,
-        )
 
     def a2a(d):
         major, minor = place(d % 2)
@@ -224,60 +241,97 @@
         major, minor = place(d % 2)
         piece = gathered.at[d, major * SIDE + minor]
         return remote(
-            piece, piece, ag1_send.at[d, j], ag1_recv.at[d, j], minor_peer(d % 2, j + 1)[1]
-        )
-
-    def ag2(d, j):
+            piece, piece, ag1_send.at[d, j], ag1_recv.at[d, j], minor_peer(d % 2, j)[1]
+        )
+
+    def ag2(d, side):
         major, minor = place(d % 2)
         piece = gathered.at[d, pl.ds(major * SIDE, SIDE)]
         return remote(
-            piece, piece, ag2_send.at[d, j], ag2_recv.at[d, j], major_peer(d % 2, j + 1)[1]
-        )
-
-    def rs1(d, j):
-        to, device = major_peer(d % 2, j + 1)
+            piece,
+            piece,
+            ag2_send.at[d, side],
+            ag2_recv.at[d, side],
+            major_peer(d % 2, 1 + 2 * side)[1],
+        )
+
+    def ag3(d, side):
+        origin = major_peer(d % 2, 3 - 2 * side)[0]
+        piece = gathered.at[d, pl.ds(origin * SIDE + 2 * side, 2)]
+        return remote(
+            piece,
+            piece,
+            ag3_send.at[d, side],
+            ag3_recv.at[d, side],
+            major_peer(d % 2, 1 + 2 * side)[1],
+        )
+
+    def rs0(d, side):
+        opposite = major_peer(d % 2, 2)[0]
+        device = major_peer(d % 2, 1 + 2 * side)[1]
+        return (
+            remote(
+                sums1.at[d, pl.ds(opposite * SIDE + 2 * side, 2)],
+                sums0_in.at[d, side],
+                rs0_send.at[d, side],
+                rs0_recv.at[d, side],
+                device,
+            ),
+            remote(
+                stats1.at[d, opposite],
+                stats0_in.at[d, side],
+                rs0s_send.at[d, side],
+                rs0s_recv.at[d, side],
+                device,
+            ),
+        )
+
+    def rs1(d, side):
+        to, device = major_peer(d % 2, 1 + 2 * side)
         return (
             remote(
                 sums1.at[d, pl.ds(to * SIDE, SIDE)],
-                sums1_in.at[d, j],
-                rs1_send.at[d, j],
-                rs1_recv.at[d, j],
+                sums1_in.at[d, side],
+                rs1_send.at[d, side],
+                rs1_recv.at[d, side],
                 device,
             ),
             remote(
                 stats1.at[d, to],
-                stats1_in.at[d, j],
-                rs1s_send.at[d, j],
-                rs1s_recv.at[d, j],
+                stats1_in.at[d, side],
+                rs1s_send.at[d, side],
+                rs1s_recv.at[d, side],
                 device,
             ),
         )
 
-    def rs2(d, j):
-        to, device = minor_peer(d % 2, j + 1)
+    def back(d, j):
+        to, device = minor_peer(d % 2, j)
+        device = ((pool + d) % POOL, device[1])
         return (
             remote(
                 sums2.at[d, to],
                 sums2_in.at[d, j],
-                rs2_send.at[d, j],
-                rs2_recv.at[d, j],
+                ret_send.at[d, j],
+                ret_recv.at[d, j],
                 device,
             ),
             remote(
                 stats2.at[d],
                 stats2_in.at[d, j],
-                rs2s_send.at[d, j],
-                rs2s_recv.at[d, j],
+                rets_send.at[d, j],
+                rets_recv.at[d, j],
                 device,
             ),
         )
 
-    def back(d):
-        device = ((pool + d) % POOL, tp)
-        return (
-            remote(sums3.at[d], sums3_in.at[d], ret_send.at[d], ret_recv.at[d], device),
-            remote(stats3.at[d], stats3_in.at[d], rets_send.at[d], rets_recv.at[d], device),
-        )
+    def each_way(d, body):
+        for j in range(1, SIDE):
+            body(j)
+
+        @pl.when(d > 0)
+        def _():
+            body(0)
 
     def packed(d):
         rows = slice(d * SHARD, (d + 1) * SHARD)
@@ -292,35 +346,56 @@
     gathered[0, major * SIDE + minor] = packed(0)
     for d in range(1, SEQ):
         outgoing[d] = packed(d)
-    pl.semaphore_wait(barrier, POOL - 1 + TP - 1)
+    pl.semaphore_wait(barrier, (POOL - 1) * SIDE + TP - 1)
     for d in range(1, SEQ):
         a2a(d).start()
 
-    def gather(i, carry):
-        @pl.when(i < SEQ)
+    def stage(d, body):
+        @pl.when((d >= 0) & (d < SEQ))
         def _():
-            @pl.when(i > 0)
-            def _():
-                a2a(i).wait_recv()
-
-            for j in range(SIDE - 1):
-                ag1(i, j).start()
-
-        @pl.when(i > 0)
+            body(d)
+
+    def first_gather(d):
+        @pl.when(d > 0)
         def _():
-            for j in range(SIDE - 1):
-                ag1(i - 1, j).wait_recv()
-            for j in range(SIDE - 1):
-                ag2(i - 1, j).start()
+            a2a(d).wait_recv()
+
+        for j in range(1, SIDE):
+            ag1(d, j).start()
+
+    def second_gather(d):
+        for j in range(1, SIDE):
+            ag1(d, j).wait_recv()
+        for side in range(2):
+            ag2(d, side).start()
+
+    def third_gather(d):
+        for side in range(2):
+            ag2(d, side).wait_recv()
+            ag3(d, side).start()
+
+    def early(i, carry):
+        stage(i + AHEAD1, first_gather)
+        stage(i + AHEAD2, second_gather)
+        stage(i + AHEAD3, third_gather)
+
+        @pl.when(i + AHEAD1 < PARTS)
+        def _():
+            for copy in cache_loads(i + AHEAD1):
+                copy.start()
 
         return carry
 
-    lax.fori_loop(0, SEQ + 1, gather, 0)
+    lax.fori_loop(-AHEAD1, 0, early, 0)
 
     loads[2].wait()
     row, col = iota((SEQ * STEPS, SEQ * STEPS), 0), iota((SEQ * STEPS, SEQ * STEPS), 1)
     pick = ((col >> 2) == slot_vector(row >> 2)) & ((col & 3) == (row & 3))
-    ordered = dot(jnp.where(pick, 1.0, 0.0).astype(BF16), fresh[...]).astype(BF16)
+    flat_fresh[...] = jnp.zeros_like(flat_fresh)
+    for k in range(SEQ):
+        flat_fresh[k * STEPS : (k + 1) * STEPS, : RANK + ROPE] = fresh[k].astype(F32)
+    flat = flat_fresh[...].astype(BF16)
+    ordered = dot(jnp.where(pick, 1.0, 0.0).astype(BF16), flat).astype(BF16)
     scores = dot_nt(absorbed[...], ordered) * SCALE
     row, col = iota(scores.shape, 0), iota(scores.shape, 1)
     causal = ((col >> 2) == (row >> 5)) & ((col & 3) <= (row & 3))
@@ -328,12 +403,15 @@
     weights = jnp.where(causal, jnp.exp(scores - top), 0.0)
     high = weights.astype(BF16)
     low = (weights - high.astype(F32)).astype(BF16)
-    fresh_sums[...] = dot(high, ordered[:, :RANK]) + dot(low, ordered[:, :RANK])
-    fresh_stats[...] = two_columns(top, jnp.sum(weights, axis=1, keepdims=True))
+    sums = dot(high, ordered[:, :RANK]) + dot(low, ordered[:, :RANK])
+    fresh_sums[...] = sums.reshape(SEQ, SHARD, RANK)
+    columns = two_columns(top, jnp.sum(weights, axis=1, keepdims=True))
+    fresh_stats[...] = columns.reshape(SEQ, SHARD, 128)
 
     rope_keys[...] = jnp.zeros_like(rope_keys)
-    loads[3].wait()
-    loads[4].wait()
+    for part in range(PARTS):
+        for copy in cache_loads(part):
+            copy.wait()
 
     def attend(d):
         target = (pool + d) % POOL
@@ -378,16 +456,42 @@
 
         lax.fori_loop(0, 2, half, 0)
 
-    def columns_of(first, others):
-        rows = [first] + [others[j] for j in range(SIDE - 1)]
-        rows.append(jnp.zeros((128 - 8 * SIDE, 128), F32))
+    def columns_of(rows):
+        rows = rows + [jnp.zeros((128 - 8 * len(rows), 128), F32)]
         return jnp.concatenate(rows, axis=0).T
+
+    def merge0(d):
+        nexts = [major_peer(d % 2, 1 + 2 * side)[0] for side in range(2)]
+        columns = columns_of(
+            [stats1[d, to] for to in nexts] + [stats0_in[d, side] for side in range(2)]
+        )
+        rows = 2 * SHARD
+        halves = []
+        for side, to in enumerate(nexts):
+            half = slice(side * rows, (side + 1) * rows)
+            piece = pl.ds(to * SIDE + 2 * side, 2)
+            parts = []
+            for index, sums in ((side, sums1[d, piece]), (side + 2, sums0_in[d, side])):
+                parts.append(
+                    (
+                        sums.reshape(rows, RANK),
+                        columns[half, 8 * index : 8 * index + 1],
+                        columns[half, 8 * index + 1 : 8 * index + 2],
+                    )
+                )
+            sums, top, total = merge(parts)
+            sums1[d, piece] = sums.astype(BF16).reshape(2, SHARD, RANK)
+            halves.append((top, total))
+        first = jnp.concatenate([two_columns(*halves[0]), columns[rows:]], axis=0)
+        stats1[d, nexts[0]] = first.T[:8]
+        kept = two_columns(columns[:rows, 8:9], columns[:rows, 9:10])
+        stats1[d, nexts[1]] = jnp.concatenate([kept, two_columns(*halves[1])], axis=0).T[:8]
 
     def merge1(d):
         major, minor = place(d % 2)
-        columns = columns_of(stats1[d, major], [stats1_in[d, j] for j in range(SIDE - 1)])
+        columns = columns_of([stats1[d, major]] + [stats1_in[d, side] for side in range(2)])
         pieces = [sums1[d, pl.ds(major * SIDE, SIDE)]]
-        pieces += [sums1_in[d, j] for j in range(SIDE - 1)]
+        pieces += [sums1_in[d, side] for side in range(2)]
         parts = []
         for j, piece in enumerate(pieces):
             parts.append(
@@ -401,78 +505,87 @@
         sums2[d] = sums.astype(BF16).reshape(SIDE, SHARD, RANK)
         stats2[d] = two_columns(top, total).T[:8]
 
+        @pl.when(d == 0)
+        def _():
+            sums2_in[0, 0] = sums2[0, minor]
+            stats2_in[0, 0] = stats2[0]
+
     def merge2(d):
         major, minor = place(d % 2)
-        columns = columns_of(stats2[d], [stats2_in[d, j] for j in range(SIDE - 1)])
+        columns = columns_of([stats2_in[d, j] for j in range(SIDE)])
         turned[...] = columns.reshape(SIDE, SHARD, 128)
         columns = turned[minor]
-        pieces = [sums2[d, minor]] + [sums2_in[d, j] for j in range(SIDE - 1)]
-        parts = []
-        for j, piece in enumerate(pieces):
-            parts.append((piece, columns[:, 8 * j : 8 * j + 1], columns[:, 8 * j + 1 : 8 * j + 2]))
+        fresh_columns = fresh_stats[d]
+        parts = [(fresh_sums[d], fresh_columns[:, 0:1], fresh_columns[:, 1:2])]
+        for j in range(SIDE):
+            parts.append(
+                (
+                    sums2_in[d, j],
+                    columns[:, 8 * j : 8 * j + 1],
+                    columns[:, 8 * j + 1 : 8 * j + 2],
+                )
+            )
         sums, top, total = merge(parts)
-        return sums.astype(BF16), two_columns(top, total)
+        mixture[d] = (sums / total).astype(BF16)
+
+    def middle(d):
+        for side in range(2):
+            ag3(d, side).wait_recv()
+        attend(d)
+        for side in range(2):
+            for copy in rs0(d, side):
+                copy.start()
+
+    def passing(d):
+        for side in range(2):
+            for copy in rs0(d, side):
+                copy.wait_recv()
+        merge0(d)
+        for side in range(2):
+            for copy in rs1(d, side):
+                copy.start()
+
+    def first_scatter(d):
+        for side in range(2):
+            for copy in rs1(d, side):
+                copy.wait_recv()
+        merge1(d)
+
+        def send(j):
+            for copy in back(d, j):
+                copy.start()
+
+        each_way(d, send)
+
+    def finish(d):
+        def wait(j):
+            for copy in back(d, j):
+                copy.wait_recv()
+
+        each_way(d, wait)
+        merge2(d)
+
+    def start_weights(h):
+        for copy in weight_loads(h):
+            copy.start()
 
     def work(i, carry):
-        @pl.when(i < SEQ)
-        def _():
-            for j in range(SIDE - 1):
-                ag2(i, j).wait_recv()
-            attend(i)
-            for j in range(SIDE - 1):
-                for copy in rs1(i, j):
-                    copy.start()
-
-        @pl.when((i >= 1) & (i < SEQ + 1))
-        def _():
-            d = i - 1
-            for j in range(SIDE - 1):
-                for copy in rs1(d, j):
-                    copy.wait_recv()
-            merge1(d)
-            for j in range(SIDE - 1):
-                for copy in rs2(d, j):
-                    copy.start()
-
-        @pl.when(i >= 2)
-        def _():
-            d = i - 2
-            for j in range(SIDE - 1):
-                for copy in rs2(d, j):
-                    copy.wait_recv()
-            sums, stats = merge2(d)
-
-            @pl.when(d == 0)
-            def _():
-                sums3_in[0] = sums
-                stats3_in[0] = stats
-
-            @pl.when(d > 0)
-            def _():
-                sums3[d] = sums
-                stats3[d] = stats
-                for copy in back(d):
-                    copy.start()
-
+        stage(i, start_weights)
+        stage(i + AHEAD1, first_gather)
+        stage(i + AHEAD2, second_gather)
+        stage(i + AHEAD3, third_gather)
+        stage(i, middle)
+        stage(i - BEHIND0, passing)
+        stage(i - BEHIND1, first_scatter)
+        stage(i - BEHIND2, finish)
         return carry
 
-    lax.fori_loop(0, SEQ + 2, work, 0)
-
-    for d in range(1, SEQ):
-        for copy in back(d):
-            copy.wait_recv()
-    columns = stats3_in[...].reshape(count, 128)
-    fresh_columns = fresh_stats[...]
-    sums, top, total = merge(
-        [
-            (sums3_in[...].reshape(count, RANK), columns[:, 0:1], columns[:, 1:2]),
-            (fresh_sums[...], fresh_columns[:, 0:1], fresh_columns[:, 1:2]),
-        ]
-    )
-    mixture = (sums / total).astype(BF16)
-    for copy in loads[5 : 5 + HEADS]:
-        copy.wait()
-    values = dot(mixture, uv[...])
+    lax.fori_loop(0, SEQ + BEHIND2, work, 0)
+
+    for h in range(HEADS):
+        for copy in weight_loads(h):
+            copy.wait()
+    values = dot(mixture[...].reshape(count, RANK), uv[...])
     row, lane = iota(values.shape, 0), iota(values.shape, 1)
     values = jnp.where((lane >> 7) == ((row >> 2) & (HEADS - 1)), values, 0.0).astype(BF16)
     row, col = iota((SEQ * STEPS, count), 0), iota((SEQ * STEPS, count), 1)
@@ -494,7 +607,6 @@
         )
 
     half = TP // 2
-    loads[5 + HEADS].wait()
 
     def project(c, carry):
         cols = pl.ds(pl.multiple_of(c * CHUNK, 128), CHUNK)
@@ -540,16 +652,22 @@
         spread_out((tp + j) % TP).wait_send()
 
     def drain(d, carry):
-        for j in range(SIDE - 1):
+        for j in range(1, SIDE):
             ag1(d, j).wait_send()
-            ag2(d, j).wait_send()
-            for copy in rs1(d, j) + rs2(d, j):
-                copy.wait_send()
 
         @pl.when(d > 0)
         def _():
             a2a(d).wait_send()
-            for copy in back(d):
+
+        def sent(j):
+            for copy in back(d, j):
+                copy.wait_send()
+
+        each_way(d, sent)
+        for side in range(2):
+            ag2(d, side).wait_send()
+            ag3(d, side).wait_send()
+            for copy in rs0(d, side) + rs1(d, side):
                 copy.wait_send()
 
         return carry
@@ -570,7 +688,6 @@
     out_weight,
 ):
     rows = SEQ * STEPS
-    fresh = jnp.pad(new_rows.reshape(rows, RANK + ROPE), ((0, 0), (0, 128 - ROPE)))
     dma = pltpu.SemaphoreType.DMA
     anywhere = pl.BlockSpec(memory_space=pl.ANY)
     scalars = pl.BlockSpec(memory_space=pltpu.SMEM)
@@ -580,8 +697,10 @@
         in_specs=[scalars] * 3 + [anywhere] * 7,
         out_specs=pl.BlockSpec(memory_space=pltpu.VMEM),
         scratch_shapes=[
-            pltpu.VMEM((rows, HEADS * (NOPE + ROPE)), BF16),
-            pltpu.VMEM((rows, RANK + 128), BF16),
+            pltpu.VMEM((SEQ, STEPS, HEADS * (NOPE + ROPE)), BF16),
+            pltpu.VMEM((SEQ, STEPS, RANK + ROPE), BF16),
+            pltpu.VMEM((rows, HEADS * (NOPE + ROPE)), F32),
+            pltpu.VMEM((rows, RANK + 128), F32),
             pltpu.VMEM((BLOCKS, ROWS, RANK), BF16),
             pltpu.VMEM((BLOCKS, ROPE, ROWS), BF16),
             pltpu.VMEM((HEADS, NOPE, RANK), BF16),
@@ -595,26 +714,25 @@
             pltpu.VMEM((3 * ROPE, KEYS), BF16),
             pltpu.VMEM((SEQ, TP, SHARD, RANK), BF16),
             pltpu.VMEM((SEQ, SIDE, 8, 128), F32),
-            pltpu.VMEM((SEQ, SIDE - 1, SIDE, SHARD, RANK), BF16),
-            pltpu.VMEM((SEQ, SIDE - 1, 8, 128), F32),
+            pltpu.VMEM((SEQ, 2, 2, SHARD, RANK), BF16),
+            pltpu.VMEM((SEQ, 2, 8, 128), F32),
+            pltpu.VMEM((SEQ, 2, SIDE, SHARD, RANK), BF16),
+            pltpu.VMEM((SEQ, 2, 8, 128), F32),
             pltpu.VMEM((SEQ, SIDE, SHARD, RANK), BF16),
             pltpu.VMEM((SEQ, 8, 128), F32),
-            pltpu.VMEM((SEQ, SIDE - 1, SHARD, RANK), BF16),
-            pltpu.VMEM((SEQ, SIDE - 1, 8, 128), F32),
+            pltpu.VMEM((SEQ, SIDE, SHARD, RANK), BF16),
+            pltpu.VMEM((SEQ, SIDE, 8, 128), F32),
             pltpu.VMEM((SIDE, SHARD, 128), F32),
-            pltpu.VMEM((SEQ, SHARD, RANK), BF16),
+            pltpu.VMEM((SEQ, SHARD, RANK), F32),
             pltpu.VMEM((SEQ, SHARD, 128), F32),
             pltpu.VMEM((SEQ, SHARD, RANK), BF16),
-            pltpu.VMEM((SEQ, SHARD, 128), F32),
-            pltpu.VMEM((SEQ * SHARD, RANK), F32),
-            pltpu.VMEM((SEQ * SHARD, 128), F32),
             pltpu.VMEM((TP, 16, CHUNK), BF16),
             pltpu.VMEM((TP, 16, CHUNK), BF16),
-            dma((6 + HEADS,)),
+            dma((3 + 2 * PARTS + 2 * HEADS,)),
         ]
         + [dma((SEQ,))] * 2
-        + [dma((SEQ, SIDE - 1))] * 12
-        + [dma((SEQ,))] * 4
+        + [dma((SEQ, SIDE))] * 6
+        + [dma((SEQ, 2))] * 12
         + [dma((TP,))] * 4,
         compiler_params=pltpu.CompilerParams(
             collective_id=0, has_side_effects=True, vmem_limit_bytes=60 << 20
@@ -623,8 +741,8 @@
         owner,
         lengths,
         pack_order.reshape(SEQ),
-        queries.reshape(rows, HEADS * (NOPE + ROPE)),
-        fresh,
+        queries,
+        new_rows,
         prefill_latent.reshape(BLOCKS, ROWS, RANK),
         prefill_rope.reshape(BLOCKS, ROPE, ROWS),
         uk_weight,

time: 126 us -> 107 us (0.85); the launches traced: 126 us -> 105 us
  Pallas kernels: 121 us -> 103 us
  local copies, waits for them, and re-layouts: 4.93 us -> 1.96 us
    pallas_call x1, Pallas kernels: 121 us -> 103 us  [on_device(): pl.pallas_call(kernel, out_shape=jax.ShapeDtypeStruct((rows, WIDTH), BF16...]
    reshape x2 -> x0, local copies, waits for them, and re-layouts: 2.36 us -> none  [the longest x1 1.56 us: on_device(): queries.reshape(rows, HEADS * (NOPE + ROPE))]
where the time goes in v2:
time: 107 us; the launch traced here: 105 us
  Pallas kernels  103 us (96%)
  local copies, waits for them, and re-layouts  1.96 us (2%)
    pallas_call x1, Pallas kernels, on_device(): pl.pallas_call(kernel, out_shape=jax.ShapeDtypeStruct((rows, WIDTH), BF16...  103 us

profile of v2, /device:TPU:9, one launch (start us, length us, event | category | flops | bytes accessed | tf_op | source)
XLA Modules:
  0.0 104.9 jit_solution(2248397084107634274)
XLA Ops:
  0.0 103.0 %shard_map.100 = bf16[32,7168]{1,0:T(8,128)(2,1)} custom-call(s32[8,8]{1,0:T(8,128)} %owner.1, s32[8,8]{1,0:T(8,128)} %lengths.1, s32[8]{0:T(128)} %bitcast.5, bf16[8,4,1536]{2,1,0:T(4,128)(2,1)} %queries_hbm.1, bf16[8,4,576]{2,1,0:T(4,128)(2,1)} %fresh_hbm.1, bf16[44,128,512]{2,1,0:T(8,128)(2,1)} %bitcast.3, bf16[44,64,128]{2,1,0:T(8,128)(2,1)} %bitcast.4, ...), custom_call_target="tpu_custom_call" | custom-call | tf_op jit(solution)/shard_map/pallas_call | solution.py:694
  103.0 2.0 %reshape.15 = bf16[8,4,7168]{2,1,0:T(4,128)(2,1)} reshape(bf16[32,7168]{1,0:T(8,128)(2,1)} %shard_map.100) | data formatting | bytes 917504 | tf_op jit(solution)/shard_map/reshape | solution.py:752

commit v3 on v2

--- a/solution.py
+++ b/solution.py
@@ -29,8 +29,8 @@
 CHUNK = 896
 SCALE = (NOPE + ROPE) ** -0.5
 PARTS = 4
-AHEAD1, AHEAD2, AHEAD3 = 5, 3, 1
-BEHIND0, BEHIND1, BEHIND2 = 1, 2, 3
+AHEAD1, AHEAD2, AHEAD3 = 5, 4, 1
+BEHIND0, BEHIND1, BEHIND2 = 1, 3, 5
 
 
 def iota(shape, dim):
@@ -454,7 +454,7 @@
                 stats1[d, i * 2 + part_index] = block.T[:8]
             return carry
 
-        lax.fori_loop(0, 2, half, 0)
+        lax.fori_loop(0, 2, half, 0, unroll=True)
 
     def columns_of(rows):
         rows = rows + [jnp.zeros((128 - 8 * len(rows), 128), F32)]
@@ -644,12 +644,6 @@
 
     for j in range(1, TP):
         spread_out((tp + j) % TP).start()
-    for j in range(1, TP):
-        collect((tp + j) % TP).wait_recv()
-
-    for j in range(1, TP):
-        scatter((tp + j) % TP).wait_send()
-        spread_out((tp + j) % TP).wait_send()
 
     def drain(d, carry):
         for j in range(1, SIDE):
@@ -673,6 +667,12 @@
         return carry
 
     lax.fori_loop(0, SEQ, drain, 0)
+    for j in range(1, TP):
+        scatter((tp + j) % TP).wait_send()
+    for j in range(1, TP):
+        collect((tp + j) % TP).wait_recv()
+    for j in range(1, TP):
+        spread_out((tp + j) % TP).wait_send()
 
 
 def on_device(

time: 107 us -> 101 us (0.944)
  Pallas kernels: 103 us -> 97.6 us
    pallas_call x1, Pallas kernels: 103 us -> 97.6 us  [on_device(): pl.pallas_call(kernel, out_shape=jax.ShapeDtypeStruct((rows, WIDTH), BF16...]
where the time goes in v3:
time: 101 us; the launch traced here: 99.6 us
  Pallas kernels  97.6 us (97%)
  local copies, waits for them, and re-layouts  1.96 us (2%)
    pallas_call x1, Pallas kernels, on_device(): pl.pallas_call(kernel, out_shape=jax.ShapeDtypeStruct((rows, WIDTH), BF16...  97.6 us

profile of v3, /device:TPU:9, one launch (start us, length us, event | category | flops | bytes accessed | tf_op | source)
XLA Modules:
  0.0 99.6 jit_solution(12379678850276737688)
XLA Ops:
  0.0 97.6 %shard_map.100 = bf16[32,7168]{1,0:T(8,128)(2,1)} custom-call(s32[8,8]{1,0:T(8,128)} %owner.1, s32[8,8]{1,0:T(8,128)} %lengths.1, s32[8]{0:T(128)} %bitcast.5, bf16[8,4,1536]{2,1,0:T(4,128)(2,1)} %queries_hbm.1, bf16[8,4,576]{2,1,0:T(4,128)(2,1)} %fresh_hbm.1, bf16[44,128,512]{2,1,0:T(8,128)(2,1)} %bitcast.3, bf16[44,64,128]{2,1,0:T(8,128)(2,1)} %bitcast.4, ...), custom_call_target="tpu_custom_call" | custom-call | tf_op jit(solution)/shard_map/pallas_call | solution.py:694
  97.6 2.0 %reshape.15 = bf16[8,4,7168]{2,1,0:T(4,128)(2,1)} reshape(bf16[32,7168]{1,0:T(8,128)(2,1)} %shard_map.100) | data formatting | bytes 917504 | tf_op jit(solution)/shard_map/reshape | solution.py:752
